TPU v7x, 32 devices: a whole 2x2x4 slice. The times are simulated.
32 devices in a mesh: dp: 4 (over z), expert: 8 (over y, x, core).
Axes of the slice: x: 2, y: 2, z: 4, core: 2. Of those that a mesh axis runs over, the one named last changes fastest.
Arguments:
- tokens: bfloat16 [4096, 768], P(('dp', 'expert')), may hold values from -6 to 6
- qkv_weight: bfloat16 [768, 2304], P(('dp', 'expert')), may hold values from -0.21875 to 0.21875
- out_weight: bfloat16 [768, 768], P(('dp', 'expert')), may hold values from -1.25 to 1.25
- router_weight: bfloat16 [768, 8], P(('dp', 'expert')), may hold values from -0.15625 to 0.15625
- norm_gains: bfloat16 [768, 2], P(('dp', 'expert')), may hold values from 0.5 to 1.5
- bias_table: float32 [32, 12], replicated, may hold values from -6 to 6
- expert_in: bfloat16 [8, 3072, 768], P('expert', 'dp'), may hold values from -0.21875 to 0.21875
- expert_out: bfloat16 [8, 3072, 768], P('expert', 'dp'), may hold values from -3 to 3
- expert_ids: int32 [4096, 1], P(('dp', 'expert')), may hold values from 0 to 7; in each aligned block of 128 rows (0 to 127, 128 to 255, ...) at most 20 rows name the same one
- seq_lengths: int32 [32, 3], P(('dp', 'expert')), may hold values from 1 to 64, 128 in all within a row
- bucket_ids: int32 [127], replicated, may hold values from 0 to 31, as said below
- cotangent: bfloat16 [4096, 768], P(('dp', 'expert')), may hold values from -6 to 6
Outputs:
- mixed_out: bfloat16 [4096, 768], P(('dp', 'expert'))
- grad_tokens: float32 [4096, 768], P(('dp', 'expert'))
- grad_qkv: float32 [768, 2304], P(('dp', 'expert'))
- grad_out: float32 [768, 768], P(('dp', 'expert'))
- grad_router: float32 [768, 8], P(('dp', 'expert'))
- grad_gains: float32 [768, 2], P(('dp', 'expert'))
- grad_table: float32 [32, 12], replicated
- grad_expert_in: float32 [8, 3072, 768], P('expert', 'dp')
- grad_expert_out: float32 [8, 3072, 768], P('expert', 'dp')
Inputs may be any that keep to these rules, and one draw needn't show every extreme that they name: `expert_ids`: in each device's 128 rows no expert is named more than 20 times, a bound that some block reaches. `seq_lengths`: each device's 3 lengths sum to 128, the largest is 64. `bucket_ids`: entry r is the bucket of relative position r - 63; every bucket occurs.
All inputs are finite; a program needn't handle non-finite values.
Results may differ from a plain program's by a relative error of at most 0.015.
Values may be sent and summed in bfloat16 or wider, within the bound.
A program may use at most 128 MiB of HBM per device.

v0:
```python
import jax
import jax.numpy as jnp
from jax import lax
from jax.sharding import PartitionSpec as P

H = 12
HD = 64
BUCKETS = 32


EPSILON = 1e-06
NEGATIVE = -1e30
PRECISE = lax.Precision.HIGHEST


def rms_parts(values, norm_gain):
    inverse = lax.rsqrt(jnp.mean(values * values, axis=-1, keepdims=True) + EPSILON)
    scaled = values * inverse
    return (scaled, inverse, scaled * norm_gain)


def rms_back(grad_normed, scaled, inverse, norm_gain):
    grad_scaled = grad_normed * norm_gain
    grad_input = inverse * (
        grad_scaled - scaled * jnp.mean(grad_scaled * scaled, axis=-1, keepdims=True)
    )
    return (grad_input, jnp.sum(grad_normed * scaled, axis=0))


def to_experts(arrived, peer_count):
    stacked, capacity, model_dim = arrived.shape
    local_count = stacked // peer_count
    grouped = arrived.reshape(peer_count, local_count, capacity, model_dim)
    return jnp.transpose(grouped, (1, 0, 2, 3)).reshape(
        local_count, peer_count * capacity, model_dim
    )


def from_experts(result, peer_count):
    local_count, rows_all, model_dim = result.shape
    capacity = rows_all // peer_count
    grouped = result.reshape(local_count, peer_count, capacity, model_dim)
    return jnp.transpose(grouped, (1, 0, 2, 3)).reshape(
        local_count * peer_count, capacity, model_dim
    )


def local(
    tokens,
    qkv_weight,
    out_weight,
    router_weight,
    norm_gains,
    bias_table,
    expert_in,
    expert_out,
    expert_ids,
    seq_lengths,
    bucket_ids,
    cotangent,
):
    qkv_full, out_full, router_full, gains_full = (
        lax.all_gather(qkv_weight, ("dp", "expert"), axis=0, tiled=True),
        lax.all_gather(out_weight, ("dp", "expert"), axis=0, tiled=True),
        lax.all_gather(router_weight, ("dp", "expert"), axis=0, tiled=True),
        lax.all_gather(norm_gains, ("dp", "expert"), axis=0, tiled=True),
    )
    row_count, model_dim = tokens.shape
    experts = router_full.shape[1]
    capacity = max(2, 5 * row_count // (4 * experts))
    peer_count = lax.axis_size("expert")
    longest = row_count // 2
    score_scale = HD ** (-0.5)
    first_gain = gains_full[:, 0].astype(jnp.float32)
    second_gain = gains_full[:, 1].astype(jnp.float32)
    token_f = tokens.astype(jnp.float32)
    scaled_one, inverse_one, normed_one = rms_parts(token_f, first_gain)
    normed_low = normed_one.astype(jnp.bfloat16)
    qkv_low = jnp.dot(normed_low, qkv_full, preferred_element_type=jnp.float32).astype(jnp.bfloat16)
    queries = qkv_low[:, :model_dim].reshape(row_count, H, HD)
    all_keys = qkv_low[:, model_dim : 2 * model_dim].reshape(row_count, H, HD)
    value_rows = qkv_low[:, 2 * model_dim :].reshape(row_count, H, HD)
    positions = jnp.arange(row_count, dtype=jnp.int32)
    seq_ends = jnp.cumsum(seq_lengths[0])
    segment = jnp.sum((positions[:, None] >= seq_ends[None, :]).astype(jnp.int32), axis=1)
    same_doc = (segment[:, None] == segment[None, :])[None]
    rel_index = jnp.clip(positions[None, :] - positions[:, None], -(longest - 1), longest - 1) + (
        longest - 1
    )
    bucket_hot = (bucket_ids[:, None] == jnp.arange(BUCKETS, dtype=jnp.int32)[None, :]).astype(
        jnp.float32
    )
    rel_bias = jnp.transpose(jnp.dot(bucket_hot, bias_table, precision=PRECISE))

    def expand(rel_vals):
        return rel_vals[:, rel_index]

    pos_bias, expand_back = jax.vjp(expand, rel_bias)

    def score_block():
        raw_score = (
            jnp.einsum("qhe,khe->hqk", queries, all_keys, preferred_element_type=jnp.float32)
            * score_scale
        )
        return jnp.where(same_doc, raw_score + pos_bias, NEGATIVE)

    scores = score_block()
    row_top = jnp.max(scores, axis=-1, keepdims=True)
    log_total = row_top + jnp.log(jnp.sum(jnp.exp(scores - row_top), axis=-1, keepdims=True))
    probs_low = jnp.exp(scores - log_total).astype(jnp.bfloat16)
    attended = jnp.einsum("hqk,khe->qhe", probs_low, value_rows, preferred_element_type=jnp.float32)
    attended = attended.reshape(row_count, model_dim).astype(jnp.bfloat16)
    residual = token_f + jnp.dot(attended, out_full, preferred_element_type=jnp.float32)
    scaled_two, inverse_two, normed_two = rms_parts(residual, second_gain)
    routed_in = normed_two.astype(jnp.bfloat16)
    logits = jnp.dot(routed_in, router_full, preferred_element_type=jnp.float32)
    exp_logits = jnp.exp(logits - jnp.max(logits, axis=-1, keepdims=True))
    route_probs = exp_logits / jnp.sum(exp_logits, axis=-1, keepdims=True)
    chosen = expert_ids[:, 0]
    picked = (chosen[:, None] == jnp.arange(experts, dtype=jnp.int32)[None, :]).astype(jnp.int32)
    slot_in = jnp.sum((jnp.cumsum(picked, axis=0) - picked) * picked, axis=-1)
    flat_slot = chosen * capacity + slot_in
    placer = (
        jnp.arange(experts * capacity, dtype=jnp.int32)[:, None] == flat_slot[None, :]
    ).astype(jnp.bfloat16)
    picked_f = picked.astype(jnp.float32)
    gate_value = jnp.sum(route_probs * picked_f, axis=-1, keepdims=True)
    send_rows = jnp.einsum(
        "st,td->sd", placer, routed_in, preferred_element_type=jnp.float32
    ).astype(jnp.bfloat16)
    arrived = lax.all_to_all(
        send_rows.reshape(experts, capacity, model_dim),
        "expert",
        split_axis=0,
        concat_axis=0,
        tiled=True,
    )
    expert_token_rows = to_experts(arrived, peer_count)
    all_rows = lax.all_gather(expert_token_rows, "dp", axis=1, tiled=True)
    before_activation = jnp.einsum(
        "aou,ahu->aoh", all_rows, expert_in, preferred_element_type=jnp.float32
    )
    act_vals, act_back = jax.vjp(jax.nn.gelu, before_activation)
    hidden_activations = act_vals.astype(jnp.bfloat16)
    partial_out = jnp.einsum(
        "ziq,zqb->zib", hidden_activations, expert_out, preferred_element_type=jnp.float32
    )
    expert_result = lax.psum_scatter(
        partial_out.astype(jnp.bfloat16), "dp", scatter_dimension=1, tiled=True
    )
    returned = lax.all_to_all(
        from_experts(expert_result, peer_count), "expert", split_axis=0, concat_axis=0, tiled=True
    )
    combined = jnp.einsum(
        "st,sd->td",
        placer,
        returned.reshape(experts * capacity, model_dim),
        preferred_element_type=jnp.float32,
    )
    mixed_out = (residual + gate_value * combined).astype(jnp.bfloat16)
    grad_mixed = cotangent.astype(jnp.float32)
    grad_gate = jnp.sum(grad_mixed * combined, axis=-1, keepdims=True)
    grad_comb = (gate_value * grad_mixed).astype(jnp.bfloat16)
    send_grads = jnp.einsum(
        "st,td->sd", placer, grad_comb, preferred_element_type=jnp.float32
    ).astype(jnp.bfloat16)
    gradient_received = to_experts(
        lax.all_to_all(
            send_grads.reshape(experts, capacity, model_dim),
            "expert",
            split_axis=0,
            concat_axis=0,
            tiled=True,
        ),
        peer_count,
    )
    grad_all = lax.all_gather(gradient_received, "dp", axis=1, tiled=True)
    grad_hidden = jnp.einsum(
        "aou,ahu->aoh", grad_all, expert_out, preferred_element_type=jnp.float32
    )
    gradient_before_activation = act_back(grad_hidden)[0].astype(jnp.bfloat16)
    grad_expert_in = jnp.einsum(
        "ieq,ieo->iqo", gradient_before_activation, all_rows, preferred_element_type=jnp.float32
    )
    grad_expert_out = jnp.einsum(
        "ieq,ieo->iqo", hidden_activations, grad_all, preferred_element_type=jnp.float32
    )
    grad_part = jnp.einsum(
        "ziq,zqb->zib", gradient_before_activation, expert_in, preferred_element_type=jnp.float32
    )
    grad_rows = lax.psum_scatter(
        grad_part.astype(jnp.bfloat16), "dp", scatter_dimension=1, tiled=True
    )
    grad_back = lax.all_to_all(
        from_experts(grad_rows, peer_count), "expert", split_axis=0, concat_axis=0, tiled=True
    )
    grad_routed = jnp.einsum(
        "st,sd->td",
        placer,
        grad_back.reshape(experts * capacity, model_dim),
        preferred_element_type=jnp.float32,
    )
    grad_logits = (grad_gate * gate_value * (picked_f - route_probs)).astype(jnp.bfloat16)
    grad_routed = grad_routed + jnp.einsum(
        "te,de->td", grad_logits, router_full, preferred_element_type=jnp.float32
    )
    grad_router = jnp.einsum(
        "td,te->de", routed_in, grad_logits, preferred_element_type=jnp.float32
    )
    grad_norm_two, gain_two_grad = rms_back(grad_routed, scaled_two, inverse_two, second_gain)
    grad_residual = grad_mixed + grad_norm_two
    grad_branch = grad_residual.astype(jnp.bfloat16)
    grad_out = jnp.einsum("td,te->de", attended, grad_branch, preferred_element_type=jnp.float32)
    grad_attended = jnp.einsum(
        "te,de->td", grad_branch, out_full, preferred_element_type=jnp.float32
    )
    grad_attended = grad_attended.astype(jnp.bfloat16).reshape(row_count, H, HD)
    scores_again = score_block()
    attn_probs = jnp.exp(scores_again - log_total)
    probs_again = attn_probs.astype(jnp.bfloat16)
    grad_values = jnp.einsum(
        "hqk,qhe->khe", probs_again, grad_attended, preferred_element_type=jnp.float32
    )
    grad_probs = jnp.einsum(
        "qhe,khe->hqk", grad_attended, value_rows, preferred_element_type=jnp.float32
    )
    grad_scores = attn_probs * (
        grad_probs - jnp.sum(grad_probs * attn_probs, axis=-1, keepdims=True)
    )
    grad_rel = expand_back(grad_scores)[0]
    grad_table = jnp.dot(jnp.transpose(bucket_hot), jnp.transpose(grad_rel), precision=PRECISE)
    grad_scores_low = grad_scores.astype(jnp.bfloat16)
    grad_queries = (
        jnp.einsum("hqk,khe->qhe", grad_scores_low, all_keys, preferred_element_type=jnp.float32)
        * score_scale
    )
    grad_keys = (
        jnp.einsum("hqk,qhe->khe", grad_scores_low, queries, preferred_element_type=jnp.float32)
        * score_scale
    )
    grad_qkv_rows = jnp.concatenate(
        [
            grad_queries.reshape(row_count, model_dim),
            grad_keys.reshape(row_count, model_dim),
            grad_values.reshape(row_count, model_dim),
        ],
        axis=1,
    ).astype(jnp.bfloat16)
    grad_qkv = jnp.einsum(
        "td,tf->df", normed_low, grad_qkv_rows, preferred_element_type=jnp.float32
    )
    grad_normed = jnp.einsum(
        "tf,df->td", grad_qkv_rows, qkv_full, preferred_element_type=jnp.float32
    )
    grad_norm_one, gain_one_grad = rms_back(grad_normed, scaled_one, inverse_one, first_gain)
    grad_tokens = grad_residual + grad_norm_one
    grad_gains = jnp.stack([gain_one_grad, gain_two_grad], axis=1)
    summed = (
        lax.psum_scatter(grad_qkv, ("dp", "expert"), scatter_dimension=0, tiled=True),
        lax.psum_scatter(grad_out, ("dp", "expert"), scatter_dimension=0, tiled=True),
        lax.psum_scatter(grad_router, ("dp", "expert"), scatter_dimension=0, tiled=True),
        lax.psum_scatter(grad_gains, ("dp", "expert"), scatter_dimension=0, tiled=True),
    )
    table_total = lax.psum(grad_table, ("dp", "expert"))
    return (
        mixed_out,
        grad_tokens,
        summed[0],
        summed[1],
        summed[2],
        summed[3],
        table_total,
        grad_expert_in,
        grad_expert_out,
    )


def solution(mesh):
    return jax.shard_map(
        local,
        mesh=mesh,
        in_specs=(
            P(("dp", "expert"), None),
            P(("dp", "expert"), None),
            P(("dp", "expert"), None),
            P(("dp", "expert"), None),
            P(("dp", "expert"), None),
            P(),
            P("expert", "dp", None),
            P("expert", "dp", None),
            P(("dp", "expert"), None),
            P(("dp", "expert"), None),
            P(),
            P(("dp", "expert"), None),
        ),
        out_specs=(
            P(("dp", "expert"), None),
            P(("dp", "expert"), None),
            P(("dp", "expert"), None),
            P(("dp", "expert"), None),
            P(("dp", "expert"), None),
            P(("dp", "expert"), None),
            P(),
            P("expert", "dp", None),
            P("expert", "dp", None),
        ),
        check_vma=False,
    )
```

profile of v0, /device:TPU:0, one launch (start us, length us, event | category | flops | bytes accessed | tf_op | source)
XLA Modules:
  0.0 523.5 jit_solution(10944577278949531604)
XLA Ops:
  8.7 43.3 %all-gather = bf16[32,24,2]{1,2,0:T(2,128)(2,1)S(1)} all-gather(bf16[1,24,2]{1,2,0:T(2,128)(2,1)} %bitcast.123), channel_id=1, replica_groups=mesh['dp'=4,'expert'=8] {'dp','expert'}, dimensions={0}, use_global_device_ids=true | all-gather | bytes 3168 | tf_op jit(solution)/shard_map/all_gather | solution.py:66
  52.1 0.8 reduce-window.8
  54.1 0.9 convolution_bitcast_fusion.2
  55.8 54.4 %gather_fusion = f32[16384,12]{1,0:T(8,128)} fusion(f32[12,127]{0,1:T(8,128)S(1)} %copy.74, s32[16384]{0:T(1024)S(1)} %broadcast_clamp_fusion), kind=kCustom, calls=%fused_computation | custom fusion | bytes 1638400 | tf_op jit(solution)/shard_map/jvp()/gather | solution.py:96
  110.2 6.7 %copy.76 = f32[128,128,12]{0,1,2:T(8,128)S(1)} copy(f32[128,128,12]{2,1,0:T(8,128)} %bitcast.99) | data formatting | bytes 1572864 | tf_op jit(solution)/shard_map/jvp()/gather | solution.py:96
  118.3 2.7 convolution_convert_fusion
  121.5 1.1 fusion.73
  123.1 6.4 %all-gather.7.cloned.1.call-done = bf16[768,768]{1,0:T(8,128)(2,1)} async-done(((bf16[24,768]{1,0:T(8,128)(2,1)}), bf16[768,768]{1,0:T(8,128)(2,1)}) %all-gather.7.cloned.1.call-update) | async-done | bytes 1179664 | tf_op jit(solution)/shard_map/all_gather | solution.py:64
  129.5 1.7 multiply_reduce_fusion.3
  131.6 0.8 reshape.264
  132.4 3.4 all-to-all-start
  135.9 41.1 %all-gather.1 = bf16[32,24,8]{1,2,0:T(8,128)(2,1)S(1)} all-gather(bf16[1,24,8]{1,2,0:T(8,128)(2,1)S(1)} %bitcast.122), channel_id=1, replica_groups=mesh['dp'=4,'expert'=8] {'dp','expert'}, dimensions={0}, use_global_device_ids=true | all-gather | bytes 12672 | tf_op jit(solution)/shard_map/all_gather | solution.py:65
  177.8 21.0 %all_gather.22 = bf16[1,640,768]{2,1,0:T(8,128)(2,1)S(1)} all-gather(bf16[1,160,768]{2,1,0:T(8,128)(2,1)} %reshape_transpose_reshape.12), channel_id=1, replica_groups=mesh['dp'=4,'expert'=8] {'dp'}, dimensions={1}, use_global_device_ids=true | all-gather | bytes 1228800 | tf_op jit(solution)/shard_map/all_gather | solution.py:139
  198.9 2.6 fusion.17
  201.5 1.3 copy-done.39
  202.8 2.3 fusion.7
  205.4 1.0 convolution_convert_fusion.3
  206.4 1.0 reshape.269
  207.4 10.4 %all_to_all.20 = bf16[8,20,768]{2,1,0:T(8,128)(2,1)} all-to-all(bf16[8,20,768]{2,1,0:T(8,128)(2,1)S(1)} %reshape.269), channel_id=1, replica_groups=mesh['dp'=4,'expert'=8] {'expert'}, dimensions={0} | all-to-all | bytes 491520 | tf_op jit(solution)/shard_map/all_to_all | solution.py:168
  217.7 1.0 reshape_transpose_reshape.14
  218.8 24.3 %all_gather.23 = bf16[1,640,768]{2,1,0:T(8,128)(2,1)S(1)} all-gather(bf16[1,160,768]{2,1,0:T(8,128)(2,1)S(1)} %reshape_transpose_reshape.14), channel_id=1, replica_groups=mesh['dp'=4,'expert'=8] {'dp'}, dimensions={1}, use_global_device_ids=true | all-gather | bytes 1228800 | tf_op jit(solution)/shard_map/all_gather | solution.py:177
  243.1 3.8 fusion.6
  246.9 0.9 copy-done.41
  247.8 1.9 fusion.8
  249.8 1.7 reshape_transpose_reshape.13
  251.5 3.7 all-to-all-start.1
  255.1 19.4 %reduce-scatter.9.cloned.1.call-done = bf16[1,160,768]{2,1,0:T(8,128)(2,1)} async-done(((bf16[1,640,768]{2,1,0:T(8,128)(2,1)}), bf16[1,160,768]{2,1,0:T(8,128)(2,1)}) %reduce-scatter.9.cloned.1.call-update) | async-done | bytes 245776 | tf_op jit(solution)/shard_map/reduce_scatter | solution.py:191
  274.6 1.7 reshape_transpose_reshape.15
  276.3 4.1 all-to-all-start.3
  281.3 1.9 fusion.38
  283.8 1.0 fusion.71
  284.8 2.9 all-to-all-done.3
  287.7 1.7 reshape.271
  289.4 1.9 multiply_reduce_fusion.1
  291.3 1.9 convert_add_fusion
  293.2 1.8 fusion.47
  295.1 1.8 convolution_convert_fusion.6
  297.5 1.1 fusion.41
  299.8 4.1 fusion.39
  304.0 1.2 copy-done.12
  305.2 3.9 convolution_bitcast_fusion.1
  309.1 2.7 convolution_bitcast_fusion
  311.9 2.1 fusion.35
  314.1 7.7 %copy.93 = f32[128,128,12]{2,1,0:T(8,128)} copy(f32[128,128,12]{0,1,2:T(8,128)S(1)} %copy-done.3) | data formatting | bytes 1572864 | tf_op jit(solution)/shard_map/mul | solution.py:227
  321.7 91.7 %scatter_custom_fusion = f32[12,127]{0,1:T(8,128)S(1)} fusion(s32[16384]{0:T(1024)S(1)} %fusion.51, f32[16384,12]{1,0:T(8,128)} %bitcast.100, f32[]{:T(128)} %constant.17.clone.1), kind=kCustom, calls=%fused_computation.92 | custom fusion | flops 196608 | bytes 6608 | tf_op jit(solution)/shard_map/transpose(jvp())/scatter-add | solution.py:96
  413.9 39.0 %all-reduce.2 = (f32[768,8]{0,1:T(8,128)S(1)}, f32[768,2]{0,1:T(2,128)S(1)}, f32[32,12]{0,1:T(8,128)}) all-reduce(f32[768,8]{0,1:T(8,128)S(1)} %fusion.70, f32[768,2]{0,1:T(2,128)S(1)} %pad_maximum_fusion.3, f32[32,12]{0,1:T(8,128)S(1)} %fusion.52), channel_id=6, replica_groups=mesh['dp'=4,'expert'=8] {'dp','expert'}, use_global_device_ids=true, to_apply=%region_19.20.clone | all-reduce | flops 8064 | bytes 64512
  454.2 0.9 fusion.34
  455.2 61.5 %reduce-scatter.11.cloned.1.call-done = f32[24,2304]{1,0:T(8,128)} async-done(((f32[768,2304]{1,0:T(8,128)}), f32[24,2304]{1,0:T(8,128)}) %reduce-scatter.11.cloned.1.call-update) | async-done | bytes 221200 | tf_op jit(solution)/shard_map/reduce_scatter | solution.py:259
  (146 shorter events, 12.6 us)
Async XLA Ops:
  7.2 195.6 %copy-start = (bf16[1,768,768]{2,1,0:T(8,128)(2,1)S(1)}, bf16[1,768,768]{2,1,0:T(8,128)(2,1)}, u32[]{:S(2)}) copy-start(bf16[1,768,768]{2,1,0:T(8,128)(2,1)} %param.19) | copy-start | bytes 3538948
  7.2 111.1 %all-gather.5.cloned.1.call-start = ((), (), s32[]{:S(2)}) async-start(), calls=%async_computation.8 | async-start | bytes 3649536 | tf_op jit(solution)/shard_map/all_gather | solution.py:63
  7.9 121.6 %all-gather.7.cloned.1.call-start = ((), (), s32[]{:S(2)}) async-start(), calls=%async_computation.9 | async-start | bytes 1216512 | tf_op jit(solution)/shard_map/all_gather | solution.py:64
  52.1 79.1 %copy-start.19 = (f32[768]{0:T(1024)}, f32[768]{0:T(1024)S(1)}, u32[]{:S(2)}) copy-start(f32[768]{0:T(1024)S(1)} %get-tuple-element.13) | copy-start | bytes 9220
  110.2 6.7 %copy-start.1 = (bf16[128,768]{1,0:T(8,128)(2,1)S(1)}, bf16[128,768]{1,0:T(8,128)(2,1)}, u32[]{:S(2)}) copy-start(bf16[128,768]{1,0:T(8,128)(2,1)} %param.12) | copy-start | bytes 589828
  110.2 6.8 %copy-start.23 = (s32[128,1]{0,1:T(1,128)S(1)}, s32[128,1]{0,1:T(1,128)}, u32[]{:S(2)}) copy-start(s32[128,1]{0,1:T(1,128)} %param.20) | copy-start | bytes 1540
  117.1 1.2 copy-start.29
  121.2 1.9 copy-start.5
  121.4 1.4 copy-start.7
  121.5 1.5 copy-start.9
  122.8 8.6 %copy-start.28 = (s32[128]{0:T(128)S(1)}, s32[128]{0:T(128)}, u32[]{:S(2)}) copy-start(s32[128]{0:T(128)} %multiply_add_fusion) | copy-start | bytes 1540
  129.5 6.3 %copy-start.36 = (bf16[24,8]{0,1:T(8,128)(2,1)S(1)}, bf16[24,8]{0,1:T(8,128)(2,1)}, u32[]{:S(2)}) copy-start(bf16[24,8]{0,1:T(8,128)(2,1)} %param.15) | copy-start | bytes 1156
  131.2 67.6 %copy-start.33 = (f32[128]{0:T(128)}, f32[128]{0:T(128)S(1)}, u32[]{:S(2)}) copy-start(f32[128]{0:T(128)S(1)} %add_rsqrt_fusion) | copy-start | bytes 1540
  132.4 44.7 %all-to-all-start = ((bf16[8,20,768]{2,1,0:T(8,128)(2,1)}), bf16[8,20,768]{2,1,0:T(8,128)(2,1)S(1)}, u32[]{:S(2)}, u32[]{:S(2)}) async-start(bf16[8,20,768]{2,1,0:T(8,128)(2,1)} %reshape.264), calls=%async_computation | async-start | bytes 589824 | tf_op jit(solution)/shard_map/all_to_all | solution.py:131
  135.8 114.0 %reduce-scatter.7.cloned.1.call-start = ((), (), s32[]{:S(2)}) async-start(), calls=%async_computation.10 | async-start | bytes 1228800 | tf_op jit(solution)/shard_map/reduce_scatter | solution.py:148
  177.1 28.0 %copy-start.18 = (bf16[768,8]{0,1:T(8,128)(2,1)}, bf16[768,8]{0,1:T(8,128)(2,1)S(1)}, u32[]{:S(2)}) copy-start(bf16[768,8]{0,1:T(8,128)(2,1)S(1)} %reshape.299) | copy-start | bytes 36868
  198.9 2.6 copy-start.11
  201.5 1.3 copy-start.39
  202.8 2.6 copy-start.24
  202.8 2.6 copy-start.4
  205.0 69.5 %reduce-scatter.9.cloned.1.call-start = ((), (), s32[]{:S(2)}) async-start(), calls=%async_computation.11 | async-start | bytes 1228800 | tf_op jit(solution)/shard_map/reduce_scatter | solution.py:191
  205.2 41.6 %copy-start.21 = (f32[128]{0:T(128)}, f32[128]{0:T(128)S(1)}, u32[]{:S(2)}) copy-start(f32[128]{0:T(128)S(1)} %get-tuple-element.31) | copy-start | bytes 1540
  205.3 41.5 %copy-start.26 = (f32[128]{0:T(128)}, f32[128]{0:T(128)S(1)}, u32[]{:S(2)}) copy-start(f32[128]{0:T(128)S(1)} %fusion.65) | copy-start | bytes 1540
  205.4 77.9 %copy-start.32 = (f32[128]{0:T(128)}, f32[128]{0:T(128)S(1)}, u32[]{:S(2)}) copy-start(f32[128]{0:T(128)S(1)} %multiply_reduce_fusion.4) | copy-start | bytes 1540
  243.1 3.8 copy-start.13
  243.1 4.8 copy-start.37
  251.5 24.8 %all-to-all-start.1 = ((bf16[8,20,768]{2,1,0:T(8,128)(2,1)}), bf16[8,20,768]{2,1,0:T(8,128)(2,1)S(1)}, u32[]{:S(2)}, u32[]{:S(2)}) async-start(bf16[8,20,768]{2,1,0:T(8,128)(2,1)} %reshape_transpose_reshape.13), calls=%async_computation.2 | async-start | bytes 589824 | tf_op jit(solution)/shard_map/all_to_all | solution.py:151
  276.3 11.4 %all-to-all-start.3 = ((bf16[8,20,768]{2,1,0:T(8,128)(2,1)}), bf16[8,20,768]{2,1,0:T(8,128)(2,1)}, u32[]{:S(2)}, u32[]{:S(2)}) async-start(bf16[8,20,768]{2,1,0:T(8,128)(2,1)} %reshape_transpose_reshape.15), calls=%async_computation.5 | async-start | bytes 589824 | tf_op jit(solution)/shard_map/all_to_all | solution.py:194
  280.4 174.8 %reduce-scatter.13.cloned.1.call-start = ((), (), s32[]{:S(2)}) async-start(), calls=%async_computation.13 | async-start | bytes 2433024 | tf_op jit(solution)/shard_map/reduce_scatter | solution.py:260
  295.0 2.1 copy-start.6
  295.0 221.6 %reduce-scatter.11.cloned.1.call-start = ((), (), s32[]{:S(2)}) async-start(), calls=%async_computation.12 | async-start | bytes 7299072 | tf_op jit(solution)/shard_map/reduce_scatter | solution.py:259
  297.1 1.4 copy-start.8
  297.4 1.5 copy-start.10
  298.5 1.3 copy-start.30
  304.0 1.2 copy-start.12
  305.2 3.9 copy-start.14
  305.2 3.9 copy-start.40
  309.1 2.8 copy-start.20
  309.1 2.8 copy-start.2
  309.1 2.8 copy-start.16
  309.1 2.8 copy-start.31
  311.9 2.1 copy-start.3
  314.0 99.5 %copy-start.38 = (s32[127]{0:T(128)S(1)}, s32[127]{0:T(128)}, u32[]{:S(2)}) copy-start(s32[127]{0:T(128)} %param.22) | copy-start | bytes 1528
  314.0 99.7 %copy-start.22 = (f32[128]{0:T(128)S(1)}, f32[128]{0:T(128)}, u32[]{:S(2)}) copy-start(f32[128]{0:T(128)} %copy-done.21) | copy-start | bytes 1540
  314.0 99.7 %copy-start.25 = (s32[128,1]{0,1:T(1,128)S(1)}, s32[128,1]{0,1:T(1,128)}, u32[]{:S(2)}) copy-start(s32[128,1]{0,1:T(1,128)} %param.20) | copy-start | bytes 1540
  314.0 99.7 %copy-start.27 = (f32[128]{0:T(128)S(1)}, f32[128]{0:T(128)}, u32[]{:S(2)}) copy-start(f32[128]{0:T(128)} %copy-done.26) | copy-start | bytes 1540
  314.0 99.7 %copy-start.35 = (f32[128]{0:T(128)S(1)}, f32[128]{0:T(128)}, u32[]{:S(2)}) copy-start(f32[128]{0:T(128)} %copy-done.34) | copy-start | bytes 1540
  314.0 140.2 %copy-start.17 = (f32[128,768]{1,0:T(8,128)S(1)}, f32[128,768]{1,0:T(8,128)}, u32[]{:S(2)}) copy-start(f32[128,768]{1,0:T(8,128)} %get-tuple-element.36) | copy-start | bytes 1179652
  (3 other events, 2.1 us)
Sparse Core Ops, SparseCore 0:
  10.9 62.7 all-gather.4
  76.6 52.8 all-gather.6
  205.2 25.9 reduce-scatter.6
  249.9 24.6 reduce-scatter.8
  295.2 95.8 reduce-scatter.12
  398.1 118.5 reduce-scatter.10
where the time goes:
time: 525 us; the launch traced here: 524 us
  blocking collectives  179 us (34%)
  other arithmetic  99.9 us (19%)
  waiting for transfers between devices  91.7 us (17%)
  local copies, waits for them, and re-layouts  85 us (16%)
  matrix products  41.5 us (8%)
  between operations  14.8 us (3%)
  starting transfers between devices  11.6 us (2%)
    scatter-add x1, other arithmetic, expand(): return rel_vals[:, rel_index]  91.7 us
    reduce_scatter x1, waiting for transfers between devices, local(): lax.psum_scatter(grad_qkv, ('dp', 'expert'), scatter_dimension=0, tiled=T...  61.5 us
    gather x2, local copies, waits for them, and re-layouts, expand(): return rel_vals[:, rel_index]  61.1 us
    all_gather x1, blocking collectives, local(): lax.all_gather(norm_gains, ('dp', 'expert'), axis=0, tiled=True)  43.3 us
    all_gather x1, blocking collectives, local(): lax.all_gather(router_weight, ('dp', 'expert'), axis=0, tiled=True)  41.1 us
    unnamed x1, blocking collectives  39 us
    all_gather x1, blocking collectives, local(): grad_all = lax.all_gather(gradient_received, 'dp', axis=1, tiled=True)  24.3 us
    all_gather x1, blocking collectives, local(): all_rows = lax.all_gather(expert_token_rows, 'dp', axis=1, tiled=True)  21 us
  transfers between devices with their start and end apart: 9, of which 4 were waited for; matrix products, arithmetic and copies ran while one was open for 39% of the time, Pallas kernels for 0%

commit v1 on v0

v1 whole, which is shorter than its diff:
```python
import functools

import jax
import jax.numpy as jnp
from jax import lax
from jax.experimental import pallas as pl
from jax.experimental.pallas import tpu as pltpu
from jax.sharding import PartitionSpec as P

H = 12
HD = 64
BUCKETS = 32
LANES = 128
EPSILON = 1e-06
NEGATIVE = -1e30
PRECISE = lax.Precision.HIGHEST
F32 = jnp.float32
BF16 = jnp.bfloat16
VMEM = pltpu.VMEM
BIG = 56 * 1024 * 1024


def mm(a, b, dims=((1,), (0,)), precision=None):
    return lax.dot_general(a, b, (dims, ((), ())), preferred_element_type=F32, precision=precision)


NT = ((1,), (1,))
TN = ((0,), (0,))


def rms_inverse(values):
    return lax.rsqrt(jnp.mean(values * values, axis=-1, keepdims=True) + EPSILON)


def placement(ids, experts, capacity):
    rows = ids.shape[0]
    picked = (ids == lax.broadcasted_iota(jnp.int32, (rows, experts), 1)).astype(F32)
    before = lax.broadcasted_iota(jnp.int32, (rows, rows), 1) < lax.broadcasted_iota(
        jnp.int32, (rows, rows), 0
    )
    earlier = mm(before.astype(BF16), picked.astype(BF16))
    slot = jnp.sum(earlier * picked, axis=-1, keepdims=True).astype(jnp.int32)
    flat = ids * capacity + slot
    place = (flat == lax.broadcasted_iota(jnp.int32, (rows, experts * capacity), 1)).astype(BF16)
    return picked, place


def forward_kernel(
    model_dim, experts, capacity,
    lens_ref, tok_ref, w_ref, gains_ref, rel_ref, ids_ref, cot_ref,
    normed_ref, qkv_ref, probs_ref, att_ref, res_ref, route_ref, send_ref,
):
    d = model_dim
    rows = tok_ref.shape[0]
    x = tok_ref[...].astype(F32)
    normed_ref[...] = (x * rms_inverse(x) * gains_ref[0:1, :]).astype(BF16)
    for c in range(0, 3 * d, 256):
        qkv_ref[:, c : c + 256] = mm(normed_ref[...], w_ref[:, c : c + 256]).astype(BF16)
    first = lens_ref[0, 0]
    second = first + lens_ref[0, 1]

    def segment(axis):
        pos = lax.broadcasted_iota(jnp.int32, (rows, rows), axis)
        return (pos >= first).astype(jnp.int32) + (pos >= second).astype(jnp.int32)

    same = segment(0) == segment(1)
    lane = lax.broadcasted_iota(jnp.int32, (rows, LANES), 1)
    for pair in range(H // 2):
        at = pair * LANES
        q = qkv_ref[:, at : at + LANES]
        k = qkv_ref[:, d + at : d + at + LANES]
        v = qkv_ref[:, 2 * d + at : 2 * d + at + LANES]
        outs = []
        for half in range(2):
            h = 2 * pair + half
            mine = (lane >= HD) if half else (lane < HD)
            bias = pltpu.roll(
                jnp.broadcast_to(rel_ref[h : h + 1, :], (rows, LANES)), 0, 1, stride=1, stride_axis=0
            )
            scores = mm(jnp.where(mine, q, jnp.zeros_like(q)), k, NT) * (HD ** (-0.5)) + bias
            scores = jnp.where(same, scores, NEGATIVE)
            e = jnp.exp(scores - jnp.max(scores, axis=-1, keepdims=True))
            p = e / jnp.sum(e, axis=-1, keepdims=True)
            probs_ref[h] = p
            outs.append(mm(p.astype(BF16), v))
        att_ref[:, at : at + LANES] = jnp.where(lane < HD, outs[0], outs[1]).astype(BF16)
    res = x + mm(att_ref[...], w_ref[:, 3 * d : 4 * d])
    res_ref[...] = res
    routed = (res * rms_inverse(res) * gains_ref[1:2, :]).astype(BF16)
    logits = mm(routed, w_ref[:, 4 * d :])[:, :experts]
    e = jnp.exp(logits - jnp.max(logits, axis=-1, keepdims=True))
    route = e / jnp.sum(e, axis=-1, keepdims=True)
    route_ref[...] = route
    picked, place = placement(ids_ref[...], experts, capacity)
    gate = jnp.sum(route * picked, axis=-1, keepdims=True)
    grad_comb = (gate * cot_ref[...].astype(F32)).astype(BF16)
    send_ref[:, :d] = mm(place, routed, TN).astype(BF16)
    send_ref[:, d:] = mm(place, grad_comb, TN).astype(BF16)


def backward_kernel(
    model_dim, experts, capacity,
    tok_ref, w_ref, gains_ref, ids_ref, cot_ref,
    normed_ref, qkv_ref, probs_ref, att_ref, res_ref, route_ref, ret_ref,
    mixed_ref, gtok_ref, grads_ref, grel_ref, grows_ref,
):
    d = model_dim
    rows = tok_ref.shape[0]
    x = tok_ref[...].astype(F32)
    g = cot_ref[...].astype(F32)
    res = res_ref[...]
    route = route_ref[...]
    picked, place = placement(ids_ref[...], experts, capacity)
    gate = jnp.sum(route * picked, axis=-1, keepdims=True)
    combined = mm(place, ret_ref[:, :d])
    mixed_ref[...] = (res + gate * combined).astype(BF16)
    grad_gate = jnp.sum(g * combined, axis=-1, keepdims=True)
    misc = w_ref.shape[1] - 4 * d
    glog = (grad_gate * gate * (picked - route)).astype(BF16)
    glog = jnp.concatenate([glog, jnp.zeros((rows, misc - experts), BF16)], axis=1)
    grouted = mm(place, ret_ref[:, d:]) + mm(glog, w_ref[:, 4 * d :], NT)
    inv2 = rms_inverse(res)
    scaled2 = res * inv2
    gain2 = gains_ref[1:2, :]
    routed = (scaled2 * gain2).astype(BF16)
    w = grouted * gain2
    gres = g + inv2 * (w - scaled2 * jnp.mean(w * scaled2, axis=-1, keepdims=True))
    col = lax.broadcasted_iota(jnp.int32, (rows, misc), 1)
    small = mm(routed, glog, TN) + mm(
        grouted * scaled2, (col == experts + 1).astype(F32), TN, PRECISE
    )
    branch = gres.astype(BF16)
    grads_ref[:, 3 * d : 4 * d] = mm(att_ref[...], branch, TN).astype(BF16)
    gatt = mm(branch, w_ref[:, 3 * d : 4 * d], NT).astype(BF16)
    lane = lax.broadcasted_iota(jnp.int32, (rows, LANES), 1)
    line = lax.broadcasted_iota(jnp.int32, (rows, LANES), 0)
    scale = HD ** (-0.5)
    for pair in range(H // 2):
        at = pair * LANES
        q = qkv_ref[:, at : at + LANES]
        k = qkv_ref[:, d + at : d + at + LANES]
        v = qkv_ref[:, 2 * d + at : 2 * d + at + LANES]
        ga = gatt[:, at : at + LANES]
        gq, gk, gv = [], [], []
        for half in range(2):
            h = 2 * pair + half
            mine = (lane >= HD) if half else (lane < HD)
            p = probs_ref[h]
            gp = mm(jnp.where(mine, ga, jnp.zeros_like(ga)), v, NT)
            gs = p * (gp - jnp.sum(p * gp, axis=-1, keepdims=True))
            low = gs.astype(BF16)
            gv.append(mm(p.astype(BF16), ga, TN))
            gq.append(mm(low, k) * scale)
            gk.append(mm(low, q, TN) * scale)
            step = 1
            while step < rows:
                turned = pltpu.roll(gs, LANES - step, 1)
                gs = jnp.where((line & step) != 0, turned, gs)
                step *= 2
            grel_ref[h : h + 1, :] = jnp.sum(gs, axis=0, keepdims=True)
        for base, two in ((0, gq), (d, gk), (2 * d, gv)):
            grows_ref[:, base + at : base + at + LANES] = jnp.where(
                lane < HD, two[0], two[1]
            ).astype(BF16)
    for c in range(0, 3 * d, 256):
        grads_ref[:, c : c + 256] = mm(normed_ref[...], grows_ref[:, c : c + 256], TN).astype(BF16)
    gnorm = mm(grows_ref[...], w_ref[:, : 3 * d], NT)
    inv1 = rms_inverse(x)
    scaled1 = x * inv1
    w = gnorm * gains_ref[0:1, :]
    gtok_ref[...] = gres + inv1 * (w - scaled1 * jnp.mean(w * scaled1, axis=-1, keepdims=True))
    small = small + mm(gnorm * scaled1, (col == experts).astype(F32), TN, PRECISE)
    grads_ref[:, 4 * d :] = small.astype(BF16)


def gather_weights(packed):
    return lax.all_gather(packed, ("dp", "expert"), axis=0, tiled=True)


def scatter_grads(grads):
    return lax.psum_scatter(grads, ("dp", "expert"), scatter_dimension=0, tiled=True).astype(F32)


def dispatch(send, experts, capacity):
    peers = lax.axis_size("expert")
    width = send.shape[1]
    arrived = lax.all_to_all(
        send.reshape(experts, capacity, width), "expert", split_axis=0, concat_axis=0, tiled=True
    )
    local_count = experts // peers
    grouped = jnp.transpose(
        arrived.reshape(peers, local_count, capacity, width), (1, 0, 2, 3)
    ).reshape(local_count, peers * capacity, width)
    return lax.all_gather(grouped, "dp", axis=1, tiled=True)


def collect(partial, experts, capacity):
    peers = lax.axis_size("expert")
    width = partial.shape[-1]
    local_count = experts // peers
    mine = lax.psum_scatter(partial, "dp", scatter_dimension=1, tiled=True)
    grouped = jnp.transpose(
        mine.reshape(local_count, peers, capacity, width), (1, 0, 2, 3)
    ).reshape(experts, capacity, width)
    back = lax.all_to_all(grouped, "expert", split_axis=0, concat_axis=0, tiled=True)
    return back.reshape(experts * capacity, width)


def local(
    tokens, qkv_weight, out_weight, router_weight, norm_gains, bias_table,
    expert_in, expert_out, expert_ids, seq_lengths, bucket_ids, cotangent,
):
    rows, d = tokens.shape
    experts = router_weight.shape[1]
    shard = qkv_weight.shape[0]
    parts = d // shard
    capacity = max(2, 5 * rows // (4 * experts))
    table_cols = -(-BUCKETS * H // shard)
    used = experts + 2 + table_cols
    misc = -(-used // LANES) * LANES
    total = 4 * d + misc

    packed = jnp.concatenate(
        [qkv_weight, out_weight, router_weight, norm_gains,
         jnp.zeros((shard, misc - experts - 2), BF16)], axis=1,
    )
    weights = gather_weights(packed)
    gains = jnp.transpose(weights[:, 4 * d + experts : 4 * d + experts + 2]).astype(F32)
    half = rows // 2
    ring = jnp.concatenate(
        [bucket_ids[half - 1 :], jnp.full((1,), -1, jnp.int32), bucket_ids[: half - 1]]
    )
    hot = (ring[None, :] == jnp.arange(BUCKETS, dtype=jnp.int32)[:, None]).astype(F32)
    rel = lax.dot_general(bias_table, hot, (((0,), (0,)), ((), ())), precision=PRECISE)

    kept_shapes = (
        jax.ShapeDtypeStruct((rows, d), BF16),
        jax.ShapeDtypeStruct((rows, 3 * d), BF16),
        jax.ShapeDtypeStruct((H, rows, rows), F32),
        jax.ShapeDtypeStruct((rows, d), BF16),
        jax.ShapeDtypeStruct((rows, d), F32),
        jax.ShapeDtypeStruct((rows, experts), F32),
        jax.ShapeDtypeStruct((experts * capacity, 2 * d), BF16),
    )
    vm = pl.BlockSpec(memory_space=VMEM)
    *kept, send = pl.pallas_call(
        functools.partial(forward_kernel, d, experts, capacity),
        out_shape=kept_shapes,
        in_specs=[pl.BlockSpec(memory_space=pltpu.SMEM)] + [vm] * 6,
        out_specs=[vm] * 7,
        compiler_params=pltpu.CompilerParams(vmem_limit_bytes=BIG),
        name="attention_forward",
    )(seq_lengths, tokens, weights, gains, rel, expert_ids, cotangent)

    both = dispatch(send, experts, capacity)
    rows_in, grad_in = both[..., :d], both[..., d:]
    pre = jnp.einsum("aou,ahu->aoh", rows_in, expert_in, preferred_element_type=F32)
    act, act_back = jax.vjp(jax.nn.gelu, pre)
    hidden = act.astype(BF16)
    grad_hidden = jnp.einsum("aou,ahu->aoh", grad_in, expert_out, preferred_element_type=F32)
    grad_pre = act_back(grad_hidden)[0].astype(BF16)
    part_out = jnp.einsum("ziq,zqb->zib", hidden, expert_out, preferred_element_type=F32)
    part_grad = jnp.einsum("ziq,zqb->zib", grad_pre, expert_in, preferred_element_type=F32)
    partial = jnp.concatenate([part_out.astype(BF16), part_grad.astype(BF16)], axis=-1)
    ret = collect(partial, experts, capacity)
    grad_expert_in = jnp.einsum("ieq,ieo->iqo", grad_pre, rows_in, preferred_element_type=F32)
    grad_expert_out = jnp.einsum("ieq,ieo->iqo", hidden, grad_in, preferred_element_type=F32)

    mixed, grad_tokens, grads, grel = pl.pallas_call(
        functools.partial(backward_kernel, d, experts, capacity),
        out_shape=(
            jax.ShapeDtypeStruct((rows, d), BF16),
            jax.ShapeDtypeStruct((rows, d), F32),
            jax.ShapeDtypeStruct((d, total), BF16),
            jax.ShapeDtypeStruct((H, LANES), F32),
        ),
        in_specs=[vm] * 12,
        out_specs=[vm] * 4,
        scratch_shapes=[VMEM((rows, 3 * d), BF16)],
        compiler_params=pltpu.CompilerParams(vmem_limit_bytes=BIG),
        name="attention_backward",
    )(tokens, weights, gains, expert_ids, cotangent, *kept, ret)

    table = lax.dot_general(hot, grel, (((1,), (1,)), ((), ())), precision=PRECISE)
    tile = jnp.pad(table.reshape(-1), (0, shard * table_cols - BUCKETS * H))
    tile = jnp.tile(tile.reshape(shard, table_cols).astype(BF16), (parts, 1))
    grads = lax.dynamic_update_slice(grads, tile, (0, 4 * d + experts + 2))
    summed = scatter_grads(grads)
    at = 4 * d + experts
    table_sum = summed[:, at + 2 : at + 2 + table_cols].reshape(-1)[: BUCKETS * H]
    return (
        mixed,
        grad_tokens,
        summed[:, : 3 * d],
        summed[:, 3 * d : 4 * d],
        summed[:, 4 * d : at],
        summed[:, at : at + 2],
        table_sum.reshape(BUCKETS, H),
        grad_expert_in,
        grad_expert_out,
    )


def solution(mesh):
    both = P(("dp", "expert"), None)
    wide = P("expert", "dp", None)
    return jax.shard_map(
        local,
        mesh=mesh,
        in_specs=(both, both, both, both, both, P(), wide, wide, both, both, P(), both),
        out_specs=(both, both, both, both, both, both, P(), wide, wide),
        check_vma=False,
    )
```

time: 525 us -> 348 us (0.66)
  blocking collectives: 179 us -> 26.9 us
  waiting for transfers between devices: 91.7 us -> 239 us
  other arithmetic: 99.9 us -> 3.19 us
  local copies, waits for them, and re-layouts: 85 us -> 24.3 us
  matrix products: 41.5 us -> 15.1 us
  Pallas kernels: 0 us -> 24.1 us
  starting transfers between devices: 11.6 us -> 0.16 us
    all_gather x4 -> x0, blocking collectives: 130 us -> none  [the longest x1 43.3 us: local(): lax.all_gather(norm_gains, ('dp', 'expert'), axis=0, tiled=True)]
    all_gather x2, waiting for transfers between devices: 6.42 us -> 105 us  [the longest x1 63.8 us: gather_weights(): return lax.all_gather(packed, ('dp', 'expert'), axis=0, tiled=True)]
    unnamed x6 -> x5, waiting for transfers between devices: 1.44 us -> 93.3 us
    scatter-add x1 -> x0, other arithmetic: 91.7 us -> none  [expand(): return rel_vals[:, rel_index]]
    gather x2 -> x0, local copies, waits for them, and re-layouts: 61.1 us -> none  [expand(): return rel_vals[:, rel_index]]
    reduce_scatter x4 -> x1, waiting for transfers between devices: 81 us -> 40.4 us  [collect(): mine = lax.psum_scatter(partial, 'dp', scatter_dimension=1, tiled=True)]
    unnamed x1 -> x0, blocking collectives: 39 us -> none
    dot_general x27 -> x8, matrix products: 41.5 us -> 15.1 us  [the longest x1 3.87 us: local(): jnp.einsum('ieq,ieo->iqo', grad_pre, rows_in, preferred_element_type=F32)]
  transfers between devices with their start and end apart: 9 -> 4, of which waited for: 4 -> 4; matrix products, arithmetic and copies ran while one was open for 39% -> 3% of each run, Pallas kernels for 0% -> 0%
where the time goes in v1:
time: 348 us; the launch traced here: 347 us
  waiting for transfers between devices  239 us (69%)
  blocking collectives  26.9 us (8%)
  local copies, waits for them, and re-layouts  24.3 us (7%)
  Pallas kernels  24.1 us (7%)
  matrix products  15.1 us (4%)
  between operations  13.9 us (4%)
    unnamed x5, waiting for transfers between devices  93.3 us
    all_gather x1, waiting for transfers between devices, gather_weights(): return lax.all_gather(packed, ('dp', 'expert'), axis=0, tiled=True)  63.8 us
    all_gather x1, waiting for transfers between devices, dispatch(): return lax.all_gather(grouped, 'dp', axis=1, tiled=True)  41.6 us
    reduce_scatter x1, waiting for transfers between devices, collect(): mine = lax.psum_scatter(partial, 'dp', scatter_dimension=1, tiled=True)  40.4 us
    pallas_call x1, Pallas kernels, local(): pl.pallas_call(functools.partial(backward_kernel, d, experts, capacity),...  15.5 us
    all_to_all x1, blocking collectives, collect(): lax.all_to_all(grouped, 'expert', split_axis=0, concat_axis=0, tiled=True)  13.9 us
    all_to_all x1, blocking collectives, dispatch(): lax.all_to_all(send.reshape(experts, capacity, width), 'expert', split_ax...  13 us
    unnamed x21, local copies, waits for them, and re-layouts  9.11 us
  transfers between devices with their start and end apart: 4, of which 4 were waited for; matrix products, arithmetic and copies ran while one was open for 3% of the time, Pallas kernels for 0%

profile of v1, /device:TPU:0, one launch (start us, length us, event | category | flops | bytes accessed | tf_op | source)
XLA Modules:
  0.0 346.7 jit_solution(2554180589420988284)
XLA Ops:
  7.2 0.0 all-gather.3.cloned.1.call-start
  7.2 0.8 copy.40
  8.1 0.7 copy.41
  8.8 1.6 concatenate.9
  10.5 0.0 all-gather.5.cloned.1.call-start
  10.6 0.7 slice.31
  11.3 1.4 copy.44.ids_ref
  12.7 0.7 pad_add_fusion
  13.4 1.4 convolution_bitcast_fusion.2.rel_ref
  14.8 63.8 %all-gather.3.cloned.1.call-done.w_ref = bf16[768,3200]{1,0:T(8,128)(2,1)} async-done(((bf16[24,3200]{1,0:T(8,128)(2,1)}), bf16[768,3200]{1,0:T(8,128)(2,1)}) %all-gather.3.cloned.1.call-update) | async-done | bytes 4915216 | tf_op jit(solution)/shard_map/all_gather | solution.py:177
  78.6 1.0 slice_convert_fusion
  79.7 0.7 copy.50
  80.4 8.6 %attention_forward.1 = (bf16[128,768]{1,0:T(8,128)(2,1)}, bf16[128,2304]{1,0:T(8,128)(2,1)}, f32[12,128,128]{2,1,0:T(8,128)}, bf16[128,768]{1,0:T(8,128)(2,1)}, ...) custom-call(s32[1,3]{1,0:T(1,128)} %lens_ref.1, bf16[128,768]{1,0:T(8,128)(2,1)} %tok_ref.3, ...), custom_call_target="tpu_custom_call" | custom-call | tf_op jit(solution)/shard_map/attention_forward/pallas_call | solution.py:246
  89.1 1.2 reshape.92
  90.3 13.0 %all_to_all.10 = bf16[8,20,1536]{2,1,0:T(8,128)(2,1)S(1)} all-to-all(bf16[8,20,1536]{2,1,0:T(8,128)(2,1)S(1)} %reshape.92), channel_id=1, replica_groups=mesh['dp'=4,'expert'=8] {'expert'}, dimensions={0} | all-to-all | bytes 983040 | tf_op jit(solution)/shard_map/all_to_all | solution.py:187
  103.3 0.9 reshape_transpose_reshape.6
  104.2 0.0 reduce-scatter.5.cloned.1.call-start
  104.2 41.6 %all-gather.5.cloned.1.call-done = bf16[1,640,1536]{2,1,0:T(8,128)(2,1)} async-done(((bf16[1,160,1536]{2,1,0:T(8,128)(2,1)}), bf16[1,640,1536]{2,1,0:T(8,128)(2,1)}) %all-gather.5.cloned.1.call-update) | async-done | bytes 1966096 | tf_op jit(solution)/shard_map/all_gather | solution.py:194
  145.8 2.2 fusion.15
  148.0 1.3 fusion.7
  149.3 0.9 copy-done.1
  150.2 1.8 fusion.6
  152.1 0.9 copy-done.6
  153.0 0.9 fusion.8
  154.0 1.4 pad_maximum_fusion
  155.4 0.0 reduce-scatter.7.cloned.1.call-start
  155.5 40.4 %reduce-scatter.5.cloned.1.call-done = bf16[1,160,1536]{2,1,0:T(8,128)(2,1)} async-done(((bf16[1,640,1536]{2,1,0:T(8,128)(2,1)}), bf16[1,160,1536]{2,1,0:T(8,128)(2,1)}) %reduce-scatter.5.cloned.1.call-update) | async-done | bytes 491536 | tf_op jit(solution)/shard_map/reduce_scatter | solution.py:201
  195.8 1.1 reshape_transpose_reshape.7
  197.0 13.9 %all_to_all.11 = bf16[8,20,1536]{2,1,0:T(8,128)(2,1)S(1)} all-to-all(bf16[8,20,1536]{2,1,0:T(8,128)(2,1)S(1)} %reshape_transpose_reshape.7), channel_id=1, replica_groups=mesh['dp'=4,'expert'=8] {'expert'}, dimensions={0} | all-to-all | bytes 983040 | tf_op jit(solution)/shard_map/all_to_all | solution.py:205
  210.9 0.9 reshape.97.ret_ref
  211.8 15.5 %attention_backward.1 = (bf16[128,768]{1,0:T(8,128)(2,1)}, f32[128,768]{1,0:T(8,128)}, bf16[768,3200]{1,0:T(8,128)(2,1)}, f32[12,128]{1,0:T(8,128)}) custom-call(bf16[128,768]{1,0:T(8,128)(2,1)} %tok_ref.3, bf16[768,3200]{1,0:T(8,128)(2,1)} %all-gather.3.cloned.1.call-done.w_ref, f32[2,768]{1,0:T(2,128)} %bitcast.39, s32[128,1]{1,0:T(8,128)} %copy.44.ids_ref, ...), custom_call_target="tpu_custom_call" | custom-call | tf_op jit(solution)/shard_map/attention_backward/pallas_call | solution.py:269
  227.2 0.8 convolution_convert_fusion.2
  228.0 0.1 copy.45
  228.1 0.1 convert_element_type.48
  228.3 3.1 dynamic_update_slice.3
  231.5 1.5 copy-done.2
  233.0 3.9 %convolution_bitcast_fusion.1 = f32[1,768,768]{2,1,0:T(8,128)} fusion(bf16[640,768]{1,0:T(8,128)(2,1)} %copy-done.6, bf16[1,640,1536]{2,1,0:T(8,128)(2,1)S(1)} %copy-done.2), kind=kOutput, calls=%fused_computation.12 | convolution fusion | flops 754974720 | bytes 4325376 | tf_op jit(solution)/shard_map/ieq,ieo->iqo/dot_general | solution.py:266
  236.9 2.8 convolution_bitcast_fusion
  239.6 93.3 %reduce-scatter.7.cloned.1.call-done = bf16[24,3200]{1,0:T(8,128)(2,1)} async-done(((bf16[768,3200]{1,0:T(8,128)(2,1)}), bf16[24,3200]{1,0:T(8,128)(2,1)}) %reduce-scatter.7.cloned.1.call-update) | async-done | bytes 153616
  332.9 0.8 slice.46
  333.6 0.6 copy.47
  334.3 0.7 slice.45
  335.0 0.7 copy.46
  335.6 0.8 slice.47
  336.4 0.1 reshape_reshape.3
  336.5 0.7 copy.48
  337.1 1.4 slice.44
  338.6 1.6 slice.43
  (17 shorter events, 0.1 us)
Async XLA Ops:
  7.2 140.8 %copy-start = (bf16[1,768,768]{2,1,0:T(8,128)(2,1)S(1)}, bf16[1,768,768]{2,1,0:T(8,128)(2,1)}, u32[]{:S(2)}) copy-start(bf16[1,768,768]{2,1,0:T(8,128)(2,1)} %param.19) | copy-start | bytes 3538948
  7.2 71.4 %all-gather.3.cloned.1.call-start = ((), (), s32[]{:S(2)}) async-start(), calls=%async_computation.4 | async-start | bytes 5068800 | tf_op jit(solution)/shard_map/all_gather | solution.py:177
  10.5 135.3 %all-gather.5.cloned.1.call-start = ((), (), s32[]{:S(2)}) async-start(), calls=%async_computation.5 | async-start | bytes 2457600 | tf_op jit(solution)/shard_map/all_gather | solution.py:194
  89.1 56.7 %copy-start.3 = (bf16[1,768,768]{2,1,0:T(8,128)(2,1)S(1)}, bf16[1,768,768]{2,1,0:T(8,128)(2,1)}, u32[]{:S(2)}) copy-start(bf16[1,768,768]{2,1,0:T(8,128)(2,1)} %param.18) | copy-start | bytes 3538948
  104.2 91.6 %reduce-scatter.5.cloned.1.call-start = ((), (), s32[]{:S(2)}) async-start(), calls=%async_computation.6 | async-start | bytes 2457600 | tf_op jit(solution)/shard_map/reduce_scatter | solution.py:201
  148.0 1.3 copy-start.4
  148.0 2.3 copy-start.1
  152.1 0.9 copy-start.6
  155.4 177.5 %reduce-scatter.7.cloned.1.call-start = ((), (), s32[]{:S(2)}) async-start(), calls=%async_computation.7 | async-start | bytes 5068800
  231.4 1.5 copy-start.2
  233.0 3.9 %copy-start.5 = (f32[640,768]{1,0:T(8,128)S(1)}, f32[640,768]{1,0:T(8,128)}, u32[]{:S(2)}) copy-start(f32[640,768]{1,0:T(8,128)} %copy-done.4) | copy-start | bytes 5898244
Sparse Core Ops, SparseCore 0:
  11.5 67.0 all-gather.2
  104.3 41.4 all-gather.4
  155.5 40.2 reduce-scatter.4
  231.6 101.2 reduce-scatter.6

commit v2 on v1

--- a/solution.py
+++ b/solution.py
@@ -173,36 +173,180 @@
     grads_ref[:, 4 * d :] = small.astype(BF16)
 
 
+CORES = 2
+MESH = pl.DeviceIdType.MESH
+
+
+def places():
+    experts_axis = lax.axis_size("expert")
+    sizes = {"dp": lax.axis_size("dp"), "chip": experts_axis // CORES, "core": CORES,
+             "expert": experts_axis}
+    e = lax.axis_index("expert")
+    here = {"dp": lax.axis_index("dp"), "chip": e // CORES, "core": lax.rem(e, CORES), "expert": e}
+    return sizes, here
+
+
+def peer_of(here, axis, other):
+    if axis == "dp":
+        return (other, here["expert"])
+    if axis == "chip":
+        return (here["dp"], other * CORES + here["core"])
+    if axis == "core":
+        return (here["dp"], here["chip"] * CORES + other)
+    return (here["dp"], other)
+
+
+def greet(sizes, here, axes):
+    barrier = pltpu.get_barrier_semaphore()
+    count = 0
+    for axis in axes:
+        for k in range(1, sizes[axis]):
+            other = lax.rem(here[axis] + k, sizes[axis])
+            pl.semaphore_signal(
+                barrier, inc=1, device_id=peer_of(here, axis, other), device_id_type=MESH
+            )
+            count += 1
+    pl.semaphore_wait(barrier, count)
+
+
+def send_all(sizes, here, axis, source, target, send_sem, recv_sem, base):
+    copies = []
+    for k in range(1, sizes[axis]):
+        other = lax.rem(here[axis] + k, sizes[axis])
+        copy = pltpu.make_async_remote_copy(
+            src_ref=source(other), dst_ref=target,
+            send_sem=send_sem.at[base + k - 1], recv_sem=recv_sem.at[base + k - 1],
+            device_id=peer_of(here, axis, other), device_id_type=MESH,
+        )
+        copy.start()
+        copies.append(copy)
+    return copies
+
+
+def weights_kernel(x_ref, out_ref, send_sem, recv_sem, own_sem):
+    sizes, here = places()
+    dp, chip, core = here["dp"], here["chip"], here["core"]
+    own = pltpu.make_async_copy(x_ref, out_ref.at[dp, chip, core], own_sem)
+    own.start()
+    greet(sizes, here, ("dp", "chip", "core"))
+    base = 0
+    for axis, part, source in (
+        ("dp", out_ref.at[dp, chip, core], x_ref),
+        ("chip", out_ref.at[:, chip, core], None),
+        ("core", out_ref.at[:, :, core], None),
+    ):
+        source = part if source is None else source
+        copies = send_all(sizes, here, axis, lambda other: source, part, send_sem, recv_sem, base)
+        if axis == "dp":
+            own.wait()
+        for copy in copies:
+            copy.wait()
+        base += sizes[axis] - 1
+
+
+def dispatch_kernel(x_ref, out_ref, send_sem, recv_sem, own_sem):
+    sizes, here = places()
+    dp, e = here["dp"], here["expert"]
+    own = pltpu.make_async_copy(x_ref.at[e], out_ref.at[dp, e], own_sem)
+    own.start()
+    greet(sizes, here, ("expert", "dp"))
+    copies = send_all(
+        sizes, here, "expert", lambda other: x_ref.at[other], out_ref.at[dp, e],
+        send_sem, recv_sem, 0,
+    )
+    own.wait()
+    for copy in copies:
+        copy.wait()
+    copies = send_all(
+        sizes, here, "dp", lambda other: out_ref.at[dp], out_ref.at[dp],
+        send_sem, recv_sem, sizes["expert"] - 1,
+    )
+    for copy in copies:
+        copy.wait()
+
+
+def exchange_kernel(axis, position, x_ref, out_ref, send_sem, recv_sem, own_sem):
+    sizes, here = places()
+    me = here[axis]
+
+    def source(other):
+        return x_ref.at[(slice(None),) * position + (other,)]
+
+    own = pltpu.make_async_copy(source(me), out_ref.at[me], own_sem)
+    own.start()
+    greet(sizes, here, (axis,))
+    copies = send_all(sizes, here, axis, source, out_ref.at[me], send_sem, recv_sem, 0)
+    own.wait()
+    for copy in copies:
+        copy.wait()
+
+
+def remote_call(kernel, x, out_shape, copies, identity, name):
+    anywhere = pl.BlockSpec(memory_space=pl.ANY)
+    return pl.pallas_call(
+        kernel,
+        out_shape=jax.ShapeDtypeStruct(out_shape, x.dtype),
+        in_specs=[anywhere],
+        out_specs=anywhere,
+        scratch_shapes=[
+            pltpu.SemaphoreType.DMA((copies,)),
+            pltpu.SemaphoreType.DMA((copies,)),
+            pltpu.SemaphoreType.DMA,
+        ],
+        compiler_params=pltpu.CompilerParams(collective_id=identity, has_side_effects=True),
+        name=name,
+    )(x)
+
+
+def exchange(x, axis, position, identity, name):
+    count = x.shape[position]
+    rest = x.shape[:position] + x.shape[position + 1 :]
+    return remote_call(
+        functools.partial(exchange_kernel, axis, position), x, (count,) + rest, count - 1,
+        identity, name,
+    )
+
+
 def gather_weights(packed):
-    return lax.all_gather(packed, ("dp", "expert"), axis=0, tiled=True)
+    data, experts_axis = lax.axis_size("dp"), lax.axis_size("expert")
+    chips = experts_axis // CORES
+    shard, total = packed.shape
+    full = remote_call(
+        weights_kernel, packed, (data, chips, CORES, shard, total),
+        data - 1 + chips - 1 + CORES - 1, 0, "gather_weights",
+    )
+    return full.reshape(data * experts_axis * shard, total)
 
 
 def scatter_grads(grads):
-    return lax.psum_scatter(grads, ("dp", "expert"), scatter_dimension=0, tiled=True).astype(F32)
+    data, experts_axis = lax.axis_size("dp"), lax.axis_size("expert")
+    chips = experts_axis // CORES
+    rows, total = grads.shape
+    x = grads.reshape(data, chips, CORES, rows // (data * experts_axis), total)
+    x = jnp.sum(exchange(x, "core", 2, 1, "grads_core").astype(F32), axis=0).astype(BF16)
+    x = jnp.sum(exchange(x, "chip", 1, 2, "grads_chip").astype(F32), axis=0).astype(BF16)
+    return jnp.sum(exchange(x, "dp", 0, 3, "grads_data").astype(F32), axis=0)
 
 
 def dispatch(send, experts, capacity):
-    peers = lax.axis_size("expert")
+    data, peers = lax.axis_size("dp"), lax.axis_size("expert")
     width = send.shape[1]
-    arrived = lax.all_to_all(
-        send.reshape(experts, capacity, width), "expert", split_axis=0, concat_axis=0, tiled=True
-    )
     local_count = experts // peers
-    grouped = jnp.transpose(
-        arrived.reshape(peers, local_count, capacity, width), (1, 0, 2, 3)
-    ).reshape(local_count, peers * capacity, width)
-    return lax.all_gather(grouped, "dp", axis=1, tiled=True)
+    both = remote_call(
+        dispatch_kernel, send.reshape(peers, local_count * capacity, width),
+        (data, peers, local_count * capacity, width), data - 1 + peers - 1, 4, "dispatch_rows",
+    )
+    grouped = jnp.moveaxis(both.reshape(data * peers, local_count, capacity, width), 1, 0)
+    return grouped.reshape(local_count, data * peers * capacity, width)
 
 
 def collect(partial, experts, capacity):
-    peers = lax.axis_size("expert")
-    width = partial.shape[-1]
-    local_count = experts // peers
-    mine = lax.psum_scatter(partial, "dp", scatter_dimension=1, tiled=True)
-    grouped = jnp.transpose(
-        mine.reshape(local_count, peers, capacity, width), (1, 0, 2, 3)
-    ).reshape(experts, capacity, width)
-    back = lax.all_to_all(grouped, "expert", split_axis=0, concat_axis=0, tiled=True)
+    data, peers = lax.axis_size("dp"), lax.axis_size("expert")
+    local_count, _, width = partial.shape
+    grouped = jnp.moveaxis(partial.reshape(local_count, data * peers, capacity, width), 0, 1)
+    grouped = grouped.reshape(data, peers, local_count * capacity, width)
+    mine = jnp.sum(exchange(grouped, "dp", 0, 5, "return_data").astype(F32), axis=0).astype(BF16)
+    back = exchange(mine, "expert", 0, 6, "return_rows")
     return back.reshape(experts * capacity, width)
 
 

time: 348 us -> 384 us (1.10)
  Pallas kernels: 24.1 us -> 325 us
  waiting for transfers between devices: 239 us -> 0 us
  blocking collectives: 26.9 us -> 0 us
  between operations: 13.9 us -> 0.83 us
  other arithmetic: 3.19 us -> 16.1 us
    pallas_call x0 -> x7, Pallas kernels: none -> 301 us  [remote_call(): pl.pallas_call(kernel, out_shape=jax.ShapeDtypeStruct(out_shape, x.dtype)...]
    all_gather x2 -> x0, waiting for transfers between devices: 105 us -> none  [the longest x1 63.8 us: gather_weights(): return lax.all_gather(packed, ('dp', 'expert'), axis=0, tiled=True)]
    unnamed x5 -> x0, waiting for transfers between devices: 93.3 us -> none
    reduce_scatter x1 -> x0, waiting for transfers between devices: 40.4 us -> none  [collect(): mine = lax.psum_scatter(partial, 'dp', scatter_dimension=1, tiled=True)]
    all_to_all x2 -> x0, blocking collectives: 26.9 us -> none  [the longest x1 13.9 us: collect(): lax.all_to_all(grouped, 'expert', split_axis=0, concat_axis=0, tiled=True)]
    reduce_sum x0 -> x4, other arithmetic: none -> 12.7 us  [the longest x1 5.44 us: scatter_grads(): jnp.sum(exchange(x, 'core', 2, 1, 'grads_core').astype(F32), axis=0)]
  transfers between devices with their start and end apart: 4 -> 0, of which waited for: 4 -> 0; matrix products, arithmetic and copies ran while one was open for 3% -> 0% of each run, Pallas kernels for 0% -> 0%
where the time goes in v2:
time: 384 us; the launch traced here: 382 us
  Pallas kernels  325 us (85%)
  local copies, waits for them, and re-layouts  23.4 us (6%)
  matrix products  17 us (4%)
  other arithmetic  16.1 us (4%)
    pallas_call x7, Pallas kernels, remote_call(): pl.pallas_call(kernel, out_shape=jax.ShapeDtypeStruct(out_shape, x.dtype)...  301 us
    pallas_call x1, Pallas kernels, local(): pl.pallas_call(functools.partial(backward_kernel, d, experts, capacity),...  15.5 us
    pallas_call x1, Pallas kernels, local(): pl.pallas_call(functools.partial(forward_kernel, d, experts, capacity), o...  8.63 us

profile of v2, /device:TPU:0, one launch (start us, length us, event | category | flops | bytes accessed | tf_op | source)
XLA Modules:
  0.0 382.0 jit_solution(3283605630461352073)
XLA Ops:
  0.7 0.8 slice.31
  1.5 0.7 pad_add_fusion
  2.2 0.8 copy.40
  3.0 0.7 copy.41
  3.7 1.4 convolution_bitcast_fusion.2.rel_ref
  5.1 1.4 copy.44.ids_ref
  6.5 1.6 concatenate.14.x_ref
  8.2 49.2 %gather_weights.1 = bf16[4,4,2,24,3200]{4,3,2,1,0:T(8,128)(2,1)} custom-call(bf16[24,3200]{1,0:T(8,128)(2,1)} %concatenate.14.x_ref), custom_call_target="tpu_custom_call" | custom-call | tf_op jit(solution)/shard_map/gather_weights/pallas_call | solution.py:286
  57.4 1.0 slice_convert_fusion
  58.5 0.7 copy.50
  59.2 8.6 %attention_forward.1 = (bf16[128,768]{1,0:T(8,128)(2,1)}, bf16[128,2304]{1,0:T(8,128)(2,1)}, f32[12,128,128]{2,1,0:T(8,128)}, bf16[128,768]{1,0:T(8,128)(2,1)}, ...) custom-call(s32[1,3]{1,0:T(1,128)} %lens_ref.1, bf16[128,768]{1,0:T(8,128)(2,1)} %tok_ref.3, ...), custom_call_target="tpu_custom_call" | custom-call | tf_op jit(solution)/shard_map/attention_forward/pallas_call | solution.py:390
  67.9 1.9 reshape.103.x_ref
  69.8 54.0 %dispatch_rows.1 = bf16[4,8,20,1536]{3,2,1,0:T(8,128)(2,1)} custom-call(bf16[8,20,1536]{2,1,0:T(8,128)(2,1)} %reshape.103.x_ref), custom_call_target="tpu_custom_call" | custom-call | tf_op jit(solution)/shard_map/dispatch_rows/pallas_call | solution.py:286
  123.8 2.7 reshape_transpose_reshape.4
  126.6 1.0 fusion.13
  127.5 0.3 copy-done.1
  127.8 0.7 copy-done.3
  128.5 1.8 fusion.6
  130.4 1.0 copy-done.5
  131.4 0.9 convolution_convert_fusion
  132.3 0.2 concatenate.17
  132.6 4.1 %convolution_convert_fusion.1 = bf16[640,768]{1,0:T(8,128)(2,1)} fusion(bf16[1,768,768]{2,1,0:T(8,128)(2,1)} %param.19, f32[640,768]{1,0:T(8,128)} %copy-done.4), kind=kOutput, calls=%fused_computation.14 | convolution fusion | flops 759889920 | bytes 4128768 | tf_op jit(solution)/shard_map/ziq,zqb->zib/dot_general | solution.py:406
  136.7 1.3 concatenate.16
  138.0 1.6 pad_maximum_fusion.x_ref
  139.6 54.7 %return_data.1 = bf16[4,8,20,1536]{3,2,1,0:T(8,128)(2,1)} custom-call(bf16[4,8,20,1536]{3,2,1,0:T(8,128)(2,1)} %pad_maximum_fusion.x_ref), custom_call_target="tpu_custom_call" | custom-call | tf_op jit(solution)/shard_map/return_data/pallas_call | solution.py:286
  194.3 3.0 reduce_sum.45.x_ref
  197.3 9.2 %return_rows.1 = bf16[8,20,1536]{2,1,0:T(8,128)(2,1)} custom-call(bf16[8,20,1536]{2,1,0:T(8,128)(2,1)} %reduce_sum.45.x_ref), custom_call_target="tpu_custom_call" | custom-call | tf_op jit(solution)/shard_map/return_rows/pallas_call | solution.py:286
  206.5 1.9 reshape.108.ret_ref
  208.5 15.5 %attention_backward.1 = (bf16[128,768]{1,0:T(8,128)(2,1)}, f32[128,768]{1,0:T(8,128)}, bf16[768,3200]{1,0:T(8,128)(2,1)}, f32[12,128]{1,0:T(8,128)}) custom-call(bf16[128,768]{1,0:T(8,128)(2,1)} %tok_ref.3, bf16[768,3200]{1,0:T(8,128)(2,1)} %bitcast.37, f32[2,768]{1,0:T(2,128)} %bitcast.41, s32[128,1]{1,0:T(8,128)} %copy.44.ids_ref, ...), custom_call_target="tpu_custom_call" | custom-call | tf_op jit(solution)/shard_map/attention_backward/pallas_call | solution.py:413
  223.9 0.8 convolution_convert_fusion.2
  224.8 0.1 copy.45
  224.9 0.1 convert_element_type.48
  225.0 3.4 dynamic_update_slice.3
  228.4 75.6 %grads_core.1 = bf16[2,4,4,24,3200]{4,3,2,1,0:T(8,128)(2,1)} custom-call(bf16[4,4,2,24,3200]{4,3,2,1,0:T(8,128)(2,1)} %bitcast.38), custom_call_target="tpu_custom_call" | custom-call | tf_op jit(solution)/shard_map/grads_core/pallas_call | solution.py:286
  304.0 5.4 %reduce_sum.46.x_ref = bf16[4,4,24,3200]{3,2,1,0:T(8,128)(2,1)} reduce(bf16[2,4,4,24,3200]{4,3,2,1,0:T(8,128)(2,1)} %grads_core.1, bf16[]{:T(256)} %constant.4.clone.1), dimensions={0}, to_apply=%region_1.2 | reduce | flops 1228800 | bytes 7372802 | tf_op jit(solution)/shard_map/reduce_sum | solution.py:326
  309.4 31.5 %grads_chip.1 = bf16[4,4,24,3200]{3,2,1,0:T(8,128)(2,1)} custom-call(bf16[4,4,24,3200]{3,2,1,0:T(8,128)(2,1)} %reduce_sum.46.x_ref), custom_call_target="tpu_custom_call" | custom-call | tf_op jit(solution)/shard_map/grads_chip/pallas_call | solution.py:286
  340.9 3.1 reduce_sum.47.x_ref
  344.0 26.4 %grads_data.1 = bf16[4,24,3200]{2,1,0:T(8,128)(2,1)} custom-call(bf16[4,24,3200]{2,1,0:T(8,128)(2,1)} %reduce_sum.47.x_ref), custom_call_target="tpu_custom_call" | custom-call | tf_op jit(solution)/shard_map/grads_data/pallas_call | solution.py:286
  370.4 1.2 convert_reduce_fusion
  371.6 0.1 slice.47
  371.6 0.1 reshape_reshape.3
  371.7 0.7 copy.48
  372.5 0.6 copy.47
  373.1 0.7 copy.46
  373.8 0.6 slice.44
  374.4 0.7 slice.43
  375.1 4.4 %convolution_bitcast_fusion = f32[1,768,768]{2,1,0:T(8,128)} fusion(bf16[1,640,1536]{2,1,0:T(8,128)(2,1)S(1)} %copy-done.2, f32[640,768]{1,0:T(8,128)} %copy-done.4), kind=kOutput, calls=%fused_computation.11 | convolution fusion | flops 759398400 | bytes 5308416 | tf_op jit(solution)/shard_map/ieq,ieo->iqo/dot_general | solution.py:411
  379.5 2.5 convolution_bitcast_fusion.1
  (15 shorter events, 0.2 us)
Async XLA Ops:
  0.6 125.9 %copy-start = (bf16[1,768,768]{2,1,0:T(8,128)(2,1)S(1)}, bf16[1,768,768]{2,1,0:T(8,128)(2,1)}, u32[]{:S(2)}) copy-start(bf16[1,768,768]{2,1,0:T(8,128)(2,1)} %param.18) | copy-start | bytes 3538948
  126.5 1.3 copy-start.1
  126.6 2.0 copy-start.3
  128.5 1.8 copy-start.4
  130.4 1.0 copy-start.5
  343.9 31.2 %copy-start.2 = (bf16[1,640,1536]{2,1,0:T(8,128)(2,1)S(1)}, bf16[1,640,1536]{2,1,0:T(8,128)(2,1)}, u32[]{:S(2)}) copy-start(bf16[1,640,1536]{2,1,0:T(8,128)(2,1)} %copy-done.1) | copy-start | bytes 5898244
  375.1 4.4 %copy-start.6 = (bf16[640,768]{1,0:T(8,128)(2,1)S(1)}, bf16[640,768]{1,0:T(8,128)(2,1)}, u32[]{:S(2)}) copy-start(bf16[640,768]{1,0:T(8,128)(2,1)} %copy-done.5) | copy-start | bytes 2949124

commit v3 on v2

--- a/solution.py
+++ b/solution.py
@@ -244,44 +244,38 @@
         base += sizes[axis] - 1
 
 
-def dispatch_kernel(x_ref, out_ref, send_sem, recv_sem, own_sem):
+def swap_kernel(axis, position, x_ref, out_ref, send_sem, recv_sem):
     sizes, here = places()
-    dp, e = here["dp"], here["expert"]
-    own = pltpu.make_async_copy(x_ref.at[e], out_ref.at[dp, e], own_sem)
+    greet(sizes, here, (axis,))
+    copies = []
+    for k in range(1, sizes[axis]):
+        other = lax.rem(here[axis] + k, sizes[axis])
+        copy = pltpu.make_async_remote_copy(
+            src_ref=x_ref.at[(slice(None),) * position + (other,)], dst_ref=out_ref.at[k - 1],
+            send_sem=send_sem.at[k - 1], recv_sem=recv_sem.at[k - 1],
+            device_id=peer_of(here, axis, other), device_id_type=MESH,
+        )
+        copy.start()
+        copies.append(copy)
+    for copy in copies:
+        copy.wait()
+
+
+def rows_kernel(x_ref, out_ref, send_sem, recv_sem, own_sem):
+    sizes, here = places()
+    e = here["expert"]
+    own = pltpu.make_async_copy(x_ref.at[e], out_ref.at[e], own_sem)
     own.start()
-    greet(sizes, here, ("expert", "dp"))
+    greet(sizes, here, ("expert",))
     copies = send_all(
-        sizes, here, "expert", lambda other: x_ref.at[other], out_ref.at[dp, e],
-        send_sem, recv_sem, 0,
+        sizes, here, "expert", lambda other: x_ref.at[other], out_ref.at[e], send_sem, recv_sem, 0
     )
     own.wait()
     for copy in copies:
         copy.wait()
-    copies = send_all(
-        sizes, here, "dp", lambda other: out_ref.at[dp], out_ref.at[dp],
-        send_sem, recv_sem, sizes["expert"] - 1,
-    )
-    for copy in copies:
-        copy.wait()
-
-
-def exchange_kernel(axis, position, x_ref, out_ref, send_sem, recv_sem, own_sem):
-    sizes, here = places()
-    me = here[axis]
-
-    def source(other):
-        return x_ref.at[(slice(None),) * position + (other,)]
-
-    own = pltpu.make_async_copy(source(me), out_ref.at[me], own_sem)
-    own.start()
-    greet(sizes, here, (axis,))
-    copies = send_all(sizes, here, axis, source, out_ref.at[me], send_sem, recv_sem, 0)
-    own.wait()
-    for copy in copies:
-        copy.wait()
-
-
-def remote_call(kernel, x, out_shape, copies, identity, name):
+
+
+def remote_call(kernel, x, out_shape, copies, identity, name, keeps_own=True):
     anywhere = pl.BlockSpec(memory_space=pl.ANY)
     return pl.pallas_call(
         kernel,
@@ -291,20 +285,28 @@
         scratch_shapes=[
             pltpu.SemaphoreType.DMA((copies,)),
             pltpu.SemaphoreType.DMA((copies,)),
-            pltpu.SemaphoreType.DMA,
-        ],
+        ] + ([pltpu.SemaphoreType.DMA] if keeps_own else []),
         compiler_params=pltpu.CompilerParams(collective_id=identity, has_side_effects=True),
         name=name,
     )(x)
 
 
-def exchange(x, axis, position, identity, name):
+def swap_sum(x, axis, position, identity, name):
+    _, here = places()
     count = x.shape[position]
     rest = x.shape[:position] + x.shape[position + 1 :]
-    return remote_call(
-        functools.partial(exchange_kernel, axis, position), x, (count,) + rest, count - 1,
-        identity, name,
-    )
+    got = remote_call(
+        functools.partial(swap_kernel, axis, position), x, (count - 1,) + rest, count - 1,
+        identity, name, keeps_own=False,
+    )
+    total = lax.dynamic_index_in_dim(x, here[axis], position, keepdims=False).astype(F32)
+    for k in range(count - 1):
+        total = total + got[k].astype(F32)
+    return total
+
+
+def swap_rows(x, identity, name):
+    return remote_call(rows_kernel, x, x.shape, x.shape[0] - 1, identity, name)
 
 
 def gather_weights(packed):
@@ -323,30 +325,29 @@
     chips = experts_axis // CORES
     rows, total = grads.shape
     x = grads.reshape(data, chips, CORES, rows // (data * experts_axis), total)
-    x = jnp.sum(exchange(x, "core", 2, 1, "grads_core").astype(F32), axis=0).astype(BF16)
-    x = jnp.sum(exchange(x, "chip", 1, 2, "grads_chip").astype(F32), axis=0).astype(BF16)
-    return jnp.sum(exchange(x, "dp", 0, 3, "grads_data").astype(F32), axis=0)
+    x = swap_sum(x, "core", 2, 1, "grads_core").astype(BF16)
+    x = swap_sum(x, "chip", 1, 2, "grads_chip").astype(BF16)
+    return swap_sum(x, "dp", 0, 3, "grads_data")
 
 
 def dispatch(send, experts, capacity):
-    data, peers = lax.axis_size("dp"), lax.axis_size("expert")
+    peers = lax.axis_size("expert")
     width = send.shape[1]
     local_count = experts // peers
-    both = remote_call(
-        dispatch_kernel, send.reshape(peers, local_count * capacity, width),
-        (data, peers, local_count * capacity, width), data - 1 + peers - 1, 4, "dispatch_rows",
-    )
-    grouped = jnp.moveaxis(both.reshape(data * peers, local_count, capacity, width), 1, 0)
-    return grouped.reshape(local_count, data * peers * capacity, width)
+    arrived = swap_rows(
+        send.reshape(peers, local_count * capacity, width), 4, "dispatch_rows"
+    )
+    grouped = jnp.moveaxis(arrived.reshape(peers, local_count, capacity, width), 1, 0)
+    grouped = grouped.reshape(local_count, peers * capacity, width)
+    return lax.all_gather(grouped, "dp", axis=1, tiled=True)
 
 
 def collect(partial, experts, capacity):
-    data, peers = lax.axis_size("dp"), lax.axis_size("expert")
+    peers = lax.axis_size("expert")
     local_count, _, width = partial.shape
-    grouped = jnp.moveaxis(partial.reshape(local_count, data * peers, capacity, width), 0, 1)
-    grouped = grouped.reshape(data, peers, local_count * capacity, width)
-    mine = jnp.sum(exchange(grouped, "dp", 0, 5, "return_data").astype(F32), axis=0).astype(BF16)
-    back = exchange(mine, "expert", 0, 6, "return_rows")
+    mine = lax.psum_scatter(partial, "dp", scatter_dimension=1, tiled=True)
+    grouped = jnp.moveaxis(mine.reshape(local_count, peers, capacity, width), 0, 1)
+    back = swap_rows(grouped.reshape(peers, local_count * capacity, width), 5, "return_rows")
     return back.reshape(experts * capacity, width)
 
 

time: 384 us -> 286 us (0.74)
  Pallas kernels: 325 us -> 144 us
  waiting for transfers between devices: 0 us -> 79.4 us
  between operations: 0.83 us -> 14.3 us
  other arithmetic: 16.1 us -> 9.58 us
    pallas_call x7 -> x6, Pallas kernels: 301 us -> 120 us  [remote_call(): pl.pallas_call(kernel, out_shape=jax.ShapeDtypeStruct(out_shape, x.dtype)...]
    all_gather x0 -> x1, waiting for transfers between devices: none -> 45.6 us  [dispatch(): return lax.all_gather(grouped, 'dp', axis=1, tiled=True)]
    reduce_scatter x0 -> x1, waiting for transfers between devices: none -> 33.8 us  [collect(): mine = lax.psum_scatter(partial, 'dp', scatter_dimension=1, tiled=True)]
    reduce_sum x4 -> x0, other arithmetic: 12.7 us -> none  [the longest x1 5.44 us: scatter_grads(): jnp.sum(exchange(x, 'core', 2, 1, 'grads_core').astype(F32), axis=0)]
    convert_element_type x0 -> x2, other arithmetic: none -> 5.77 us  [the longest x1 3 us: scatter_grads(): x = swap_sum(x, 'core', 2, 1, 'grads_core').astype(BF16)]
  transfers between devices with their start and end apart: 0 -> 2, of which waited for: 0 -> 2; matrix products, arithmetic and copies ran while one was open for 0% -> 2% of each run, Pallas kernels for 0% -> 0%
where the time goes in v3:
time: 286 us
  Pallas kernels  144 us (50%)
  waiting for transfers between devices  79.4 us (28%)
  local copies, waits for them, and re-layouts  23.7 us (8%)
  matrix products  14.4 us (5%)
  between operations  14.3 us (5%)
  other arithmetic  9.58 us (3%)
    pallas_call x6, Pallas kernels, remote_call(): pl.pallas_call(kernel, out_shape=jax.ShapeDtypeStruct(out_shape, x.dtype)...  120 us
    all_gather x1, waiting for transfers between devices, dispatch(): return lax.all_gather(grouped, 'dp', axis=1, tiled=True)  45.6 us
    reduce_scatter x1, waiting for transfers between devices, collect(): mine = lax.psum_scatter(partial, 'dp', scatter_dimension=1, tiled=True)  33.8 us
    pallas_call x1, Pallas kernels, local(): pl.pallas_call(functools.partial(backward_kernel, d, experts, capacity),...  15.6 us
    pallas_call x1, Pallas kernels, local(): pl.pallas_call(functools.partial(forward_kernel, d, experts, capacity), o...  8.64 us
    unnamed x29, local copies, waits for them, and re-layouts  7.48 us
  transfers between devices with their start and end apart: 2, of which 2 were waited for; matrix products, arithmetic and copies ran while one was open for 2% of the time, Pallas kernels for 0%

profile of v3, /device:TPU:0, one launch (start us, length us, event | category | flops | bytes accessed | tf_op | source)
XLA Modules:
  0.0 285.8 jit_solution(589251536656713062)
XLA Ops:
  7.2 0.8 copy.34
  8.1 0.7 copy.35
  8.8 1.6 concatenate.9.x_ref
  10.5 49.2 %gather_weights.1 = bf16[4,4,2,24,3200]{4,3,2,1,0:T(8,128)(2,1)} custom-call(bf16[24,3200]{1,0:T(8,128)(2,1)} %concatenate.9.x_ref), custom_call_target="tpu_custom_call" | custom-call | tf_op jit(solution)/shard_map/gather_weights/pallas_call | solution.py:280
  59.7 1.0 slice_convert_fusion
  60.8 0.7 copy.48
  61.5 0.7 copy.38.ids_ref
  62.3 0.1 slice.49
  62.3 0.1 pad_add_fusion
  62.4 0.7 convolution_bitcast_fusion.2.rel_ref
  63.1 8.6 %attention_forward.1 = (bf16[128,768]{1,0:T(8,128)(2,1)}, bf16[128,2304]{1,0:T(8,128)(2,1)}, f32[12,128,128]{2,1,0:T(8,128)}, bf16[128,768]{1,0:T(8,128)(2,1)}, ...) custom-call(s32[1,3]{1,0:T(1,128)} %lens_ref.1, bf16[128,768]{1,0:T(8,128)(2,1)} %tok_ref.3, ...), custom_call_target="tpu_custom_call" | custom-call | tf_op jit(solution)/shard_map/attention_forward/pallas_call | solution.py:391
  71.8 2.0 reshape.118.x_ref
  73.8 10.2 %dispatch_rows.1 = bf16[8,20,1536]{2,1,0:T(8,128)(2,1)} custom-call(bf16[8,20,1536]{2,1,0:T(8,128)(2,1)} %reshape.118.x_ref), custom_call_target="tpu_custom_call" | custom-call | tf_op jit(solution)/shard_map/dispatch_rows/pallas_call | solution.py:280
  84.1 1.9 reshape_transpose_reshape.6
  86.0 0.2 reduce-scatter.2.cloned.1.call-start
  86.3 45.6 %all-gather.2.cloned.1.call-done = bf16[1,640,1536]{2,1,0:T(8,128)(2,1)} async-done(((bf16[1,160,1536]{2,1,0:T(8,128)(2,1)}), bf16[1,640,1536]{2,1,0:T(8,128)(2,1)}) %all-gather.2.cloned.1.call-update) | async-done | bytes 1966096 | tf_op jit(solution)/shard_map/all_gather | solution.py:342
  131.8 2.2 fusion.17
  134.0 1.3 fusion.8
  135.4 0.9 copy-done.5
  136.3 1.8 fusion.7
  138.2 0.9 fusion.9
  139.1 1.5 pad_maximum_fusion
  140.6 3.9 %convolution_bitcast_fusion.1 = f32[1,768,768]{2,1,0:T(8,128)} fusion(bf16[640,768]{1,0:T(8,128)(2,1)} %copy-done.10, bf16[1,640,1536]{2,1,0:T(8,128)(2,1)S(1)} %copy-done.5), kind=kOutput, calls=%fused_computation.15 | convolution fusion | flops 754974720 | bytes 4325376 | tf_op jit(solution)/shard_map/ieq,ieo->iqo/dot_general | solution.py:411
  144.5 2.7 convolution_bitcast_fusion
  147.3 33.8 %reduce-scatter.2.cloned.1.call-done = bf16[1,160,1536]{2,1,0:T(8,128)(2,1)} async-done(((bf16[1,640,1536]{2,1,0:T(8,128)(2,1)}), bf16[1,160,1536]{2,1,0:T(8,128)(2,1)}) %reduce-scatter.2.cloned.1.call-update) | async-done | bytes 491536 | tf_op jit(solution)/shard_map/reduce_scatter | solution.py:348
  181.1 2.0 reshape_transpose_reshape.7.x_ref
  183.0 9.7 %return_rows.1 = bf16[8,20,1536]{2,1,0:T(8,128)(2,1)} custom-call(bf16[8,20,1536]{2,1,0:T(8,128)(2,1)} %reshape_transpose_reshape.7.x_ref), custom_call_target="tpu_custom_call" | custom-call | tf_op jit(solution)/shard_map/return_rows/pallas_call | solution.py:280
  192.7 2.0 reshape.123.ret_ref
  194.7 15.6 %attention_backward.1 = (bf16[128,768]{1,0:T(8,128)(2,1)}, f32[128,768]{1,0:T(8,128)}, bf16[768,3200]{1,0:T(8,128)(2,1)}, f32[12,128]{1,0:T(8,128)}) custom-call(bf16[128,768]{1,0:T(8,128)(2,1)} %tok_ref.3, bf16[768,3200]{1,0:T(8,128)(2,1)} %bitcast.63, f32[2,768]{1,0:T(2,128)} %bitcast.68, s32[128,1]{1,0:T(8,128)} %copy.38.ids_ref, ...), custom_call_target="tpu_custom_call" | custom-call | tf_op jit(solution)/shard_map/attention_backward/pallas_call | solution.py:414
  210.3 0.8 convolution_convert_fusion.2
  211.1 0.1 copy.39
  211.2 0.1 convert_element_type.103
  211.4 3.1 %dynamic_update_slice.3 = bf16[768,3200]{1,0:T(8,128)(2,1)} dynamic-update-slice(bf16[768,3200]{1,0:T(8,128)(2,1)} %get-tuple-element.29, bf16[768,16]{1,0:T(8,128)(2,1)S(1)} %bitcast.66, s32[]{:T(128)} %constant.47.clone.1, s32[]{:T(128)} %constant.48.clone.1) | dynamic-update-slice | bytes 49156 | tf_op jit(solution)/shard_map/dynamic_update_slice | solution.py:432
  214.5 5.6 %grads_core.1 = bf16[1,4,4,24,3200]{4,3,2,1,0:T(8,128)(2,1)} custom-call(bf16[4,4,2,24,3200]{4,3,2,1,0:T(8,128)(2,1)} %bitcast.64), custom_call_target="tpu_custom_call" | custom-call | tf_op jit(solution)/shard_map/grads_core/pallas_call | solution.py:280
  220.1 3.0 %fusion = bf16[4,4,24,3200]{3,2,0,1:T(8,128)(2,1)S(1)} fusion(bf16[1,4,4,24,3200]{4,3,2,1,0:T(8,128)(2,1)} %grads_core.1, bf16[4,4,2,24,3200]{4,3,2,1,0:T(8,128)(2,1)} %bitcast.65, s32[]{:T(128)S(6)} %select_n.17), kind=kLoop, calls=%fused_computation.1 | loop fusion | flops 4915200 | bytes 7372804 | tf_op jit(solution)/shard_map/convert_element_type | solution.py:328
  223.1 1.5 copy-done.1
  224.5 1.6 copy.42.x_ref
  226.2 30.6 %grads_chip.1 = bf16[3,4,24,3200]{3,2,1,0:T(8,128)(2,1)} custom-call(bf16[4,4,24,3200]{3,2,1,0:T(8,128)(2,1)} %copy.42.x_ref), custom_call_target="tpu_custom_call" | custom-call | tf_op jit(solution)/shard_map/grads_chip/pallas_call | solution.py:280
  256.8 2.8 fusion.10.x_ref
  259.5 14.7 %grads_data.1 = bf16[3,24,3200]{2,1,0:T(8,128)(2,1)} custom-call(bf16[4,24,3200]{2,1,0:T(8,128)(2,1)} %fusion.10.x_ref), custom_call_target="tpu_custom_call" | custom-call | tf_op jit(solution)/shard_map/grads_data/pallas_call | solution.py:280
  274.2 1.2 add_bitcast_fusion
  275.4 0.7 slice.67
  276.1 0.6 slice.68
  276.8 0.1 slice.71
  276.8 0.1 slice.70
  277.0 0.7 copy.45
  277.7 0.7 copy.43
  278.3 0.6 copy.44
  (27 shorter events, 0.2 us)
Async XLA Ops:
  7.2 126.8 %copy-start = (bf16[1,768,768]{2,1,0:T(8,128)(2,1)S(1)}, bf16[1,768,768]{2,1,0:T(8,128)(2,1)}, u32[]{:S(2)}) copy-start(bf16[1,768,768]{2,1,0:T(8,128)(2,1)} %param.19) | copy-start | bytes 3538948
  7.2 124.6 %all-gather.2.cloned.1.call-start = ((), (), s32[]{:S(2)}) async-start(), calls=%async_computation.1 | async-start | bytes 2457600 | tf_op jit(solution)/shard_map/all_gather | solution.py:342
  10.5 51.0 %copy-start.3 = (s32[128,1]{0,1:T(1,128)S(1)}, s32[128,1]{0,1:T(1,128)}, u32[]{:S(2)}) copy-start(s32[128,1]{0,1:T(1,128)} %param.20) | copy-start | bytes 1540
  10.5 51.8 %copy-start.4 = (s32[127]{0:T(128)S(1)}, s32[127]{0:T(128)}, u32[]{:S(2)}) copy-start(s32[127]{0:T(128)} %param.22) | copy-start | bytes 1528
  10.5 51.9 %copy-start.2 = (f32[32,12]{0,1:T(8,128)S(1)}, f32[32,12]{0,1:T(8,128)}, u32[]{:S(2)}) copy-start(f32[32,12]{0,1:T(8,128)} %param.17) | copy-start | bytes 4612
  71.8 60.1 %copy-start.6 = (bf16[1,768,768]{2,1,0:T(8,128)(2,1)S(1)}, bf16[1,768,768]{2,1,0:T(8,128)(2,1)}, u32[]{:S(2)}) copy-start(bf16[1,768,768]{2,1,0:T(8,128)(2,1)} %param.18) | copy-start | bytes 3538948
  86.0 95.0 %reduce-scatter.2.cloned.1.call-start = ((), (), s32[]{:S(2)}) async-start(), calls=%async_computation.2 | async-start | bytes 2457600 | tf_op jit(solution)/shard_map/reduce_scatter | solution.py:348
  134.0 1.3 copy-start.8
  134.0 2.3 copy-start.5
  136.3 1.9 copy-start.7
  138.1 1.0 copy-start.10
  140.6 3.9 %copy-start.9 = (f32[640,768]{1,0:T(8,128)S(1)}, f32[640,768]{1,0:T(8,128)}, u32[]{:S(2)}) copy-start(f32[640,768]{1,0:T(8,128)} %copy-done.8) | copy-start | bytes 5898244
  223.1 1.5 copy-start.1
Sparse Core Ops, SparseCore 0:
  86.1 45.6 all-gather.1
  140.7 40.2 reduce-scatter.1
